TPU v7x, 32 devices: a whole 2x2x4 slice. The times are simulated.
32 devices in a mesh: groups: 2 (over y), gx: 4 (over z), gz: 2 (over x), vert: 2 (over core).
Axes of the slice: x: 2, y: 2, z: 4, core: 2. Of those that a mesh axis runs over, the one named last changes fastest.
Arguments:
- flow_field: bfloat16 [4, 4, 5, 4, 256, 256], P('groups', 'vert', None, 'gx', None, 'gz'), parts along dimension 0, may hold values from -6 to 6
- test_streams: int32 [4], P('groups'), parts along dimension 0, may hold values from 0 to 999999
- snapshot_ids: int32 [4, 4], P('groups', 'vert'), parts along dimension 0, may hold values from 0 to 65535
Outputs:
- sketch_x: float32 [8, 128], P(('groups', 'gx')), parts along dimension 0
- sketch_y: float32 [512, 128], P(('groups', 'gx', 'gz', 'vert')), parts along dimension 0
- sketch_z: float32 [512, 128], P(('groups', 'gz'), ('gx', 'vert')), parts along dimension 0
- core_sketch: float32 [4608, 2, 48], P(('groups', 'gx')), parts along dimension 0
There are 2 independent parts, one for each index of `groups`. A program takes and returns all parts, laid end to end along the dimension named above; each array names one. Nothing has to cross between parts.
All inputs are finite; a program needn't handle non-finite values.
Results may differ from a plain program's by a relative error of at most 0.007.
Values sent between devices are 32-bit elements; how exact they have to be, the bound alone decides.
A program may use at most 64 MiB of HBM per device.

v0:
```python
import math

import jax
import jax.numpy as jnp
from jax import lax
from jax.sharding import PartitionSpec as P

K = 128
S = 48
E = 2


def hash_index(index, stream, salt):
    mixed = index * -1640531535 + stream * -2048144777 + salt
    mixed = jnp.bitwise_xor(mixed, lax.shift_right_logical(mixed, jnp.int32(16)))
    mixed = mixed * 739982445
    mixed = jnp.bitwise_xor(mixed, lax.shift_right_logical(mixed, jnp.int32(13)))
    mixed = mixed * 695872825
    return jnp.bitwise_xor(mixed, lax.shift_right_logical(mixed, jnp.int32(16)))


def unit_value(index, stream, salt):
    upper = lax.shift_right_logical(hash_index(index, stream, salt), jnp.int32(9))
    return ((2 * upper + 1).astype(jnp.float32) * 2.0 ** (-24) - 1.0).astype(jnp.bfloat16)


def test_table(row_ids, col_ids, stride, stream, salt):
    return unit_value(row_ids[:, None] * stride + col_ids[None, :], stream, salt)


def shards(flow_field, test_streams, snapshot_ids):
    highest = lax.Precision.HIGHEST
    batches, local_snaps, variables, cells_x, cells_y, cells_z = flow_field.shape
    slabs_x = lax.axis_size("gx")
    total_x = cells_x * slabs_x
    total_z = cells_z * lax.axis_size("gz")
    total_q = variables * batches * local_snaps * lax.axis_size("vert")
    factor_stream = test_streams[0]
    core_stream = test_streams[1]
    rank_ids = jnp.arange(K, dtype=jnp.int32)
    sketch_ids = jnp.arange(S, dtype=jnp.int32)
    x_ids = lax.axis_index("gx") * cells_x + jnp.arange(cells_x, dtype=jnp.int32)
    y_ids = jnp.arange(cells_y, dtype=jnp.int32)
    z_ids = lax.axis_index("gz") * cells_z + jnp.arange(cells_z, dtype=jnp.int32)
    ax_tab = test_table(x_ids, rank_ids, K, factor_stream, 1).astype(jnp.float32)
    ay_low = test_table(y_ids, rank_ids, K, factor_stream, 2)
    az_low = test_table(z_ids, rank_ids, K, factor_stream, 3)
    ay_tab = ay_low.astype(jnp.float32)
    phy_low = test_table(sketch_ids, y_ids, cells_y, core_stream, 6)
    phz_low = test_table(sketch_ids, z_ids, total_z, core_stream, 7)

    def batch_terms(batch_idx):
        blocks = flow_field[batch_idx].reshape(-1, cells_x, cells_y, cells_z)
        pairs = blocks.shape[0]
        q_ids = (
            snapshot_ids[batch_idx][:, None] * variables
            + jnp.arange(variables, dtype=jnp.int32)[None, :]
        ).reshape(-1)
        aq_tab = test_table(q_ids, rank_ids, K, factor_stream, 4).astype(jnp.float32)
        phq_low = test_table(q_ids, jnp.arange(E, dtype=jnp.int32), E, core_stream, 8)
        rows_z = blocks.reshape(-1, cells_z)
        along_z = jnp.dot(rows_z, az_low, preferred_element_type=jnp.float32).reshape(
            pairs, cells_x, cells_y, K
        )
        along_y = jnp.einsum("qxyz,yk->qxzk", blocks, ay_low, preferred_element_type=jnp.float32)
        weights = aq_tab[:, None, :] * ax_tab[None, :, :]
        part_x = jnp.sum(
            jnp.sum(along_z * ay_tab[None, None, :, :], axis=2) * aq_tab[:, None, :], axis=0
        )
        part_y = jnp.sum(along_z * weights[:, :, None, :], axis=(0, 1))
        part_z = jnp.sum(along_y * weights[:, :, None, :], axis=(0, 1))
        first = jnp.dot(rows_z, phz_low.T, preferred_element_type=jnp.float32).reshape(
            pairs, cells_x, cells_y, S
        )
        second = jnp.einsum("qxyc,by->qxbc", first, phy_low.astype(jnp.float32), precision=highest)
        partial_core = jnp.einsum(
            "qxbc,qe->bcex", second, phq_low.astype(jnp.float32), precision=highest
        )
        return (part_x, part_y, part_z, partial_core.reshape(S * S, E, cells_x))

    def finish(part_x, part_y, part_z, partial_core):
        summed, sum_x = lax.psum((partial_core, part_x), ("gz", "vert"))
        phx_whole = test_table(
            sketch_ids, jnp.arange(total_x, dtype=jnp.int32), total_x, core_stream, 5
        ).astype(jnp.float32)
        core = jnp.einsum(
            "rex,ax->rea",
            lax.all_to_all(summed, "gx", split_axis=0, concat_axis=2, tiled=True),
            phx_whole,
            precision=highest,
        )
        sum_z = lax.psum_scatter(part_z, ("gx", "vert"), scatter_dimension=1, tiled=True)
        sum_y = lax.psum_scatter(part_y, ("gx", "gz", "vert"), scatter_dimension=0, tiled=True)
        return (sum_x, sum_y, sum_z, core)

    terms = [batch_terms(batch_idx) for batch_idx in range(batches)]
    totals = finish(terms[0][0], terms[0][1], terms[0][2], terms[0][3])
    for later in terms[1:]:
        latest = finish(later[0], later[1], later[2], later[3])
        totals = tuple((earlier + newer for earlier, newer in zip(totals, latest)))
    scale_x = 3.0**1.5 / math.sqrt(cells_y * total_z * total_q)
    scale_y = 3.0**1.5 / math.sqrt(total_x * total_z * total_q)
    scale_z = 3.0**1.5 / math.sqrt(total_x * cells_y * total_q)
    scale_core = 9.0 / math.sqrt(total_x * cells_y * total_z * total_q)
    return (totals[0] * scale_x, totals[1] * scale_y, totals[2] * scale_z, totals[3] * scale_core)


def solution(mesh):
    in_specs = (P("groups", "vert", None, "gx", None, "gz"), P("groups"), P("groups", "vert"))
    out_specs = (
        P(("groups", "gx"), None),
        P(("groups", "gx", "gz", "vert"), None),
        P(("groups", "gz"), ("gx", "vert")),
        P(("groups", "gx"), None, None),
    )
    return jax.shard_map(shards, mesh=mesh, in_specs=in_specs, out_specs=out_specs, check_vma=False)
```

profile of v0, /device:TPU:0, one launch (start us, length us, event | category | flops | bytes accessed | tf_op | source)
XLA Modules:
  0.0 124.9 jit_solution(1838660358389235373)
XLA Ops:
  7.2 1.3 %fusion.295 = (s32[1]{0:T(128)}, s32[1]{0:T(128)}) fusion(s32[2]{0:T(128)} %param.4), kind=kLoop, calls=%fused_computation.343 | loop fusion | bytes 16 | tf_op jit(solution)/shard_map/slice | solution.py:39
  8.5 0.8 multiply_bitcast_fusion
  9.4 0.1 mul.691
  9.5 0.1 mul.680
  9.6 1.4 %fusion.294 = (bf16[1,2,5,1,256,128]{5,4,3,2,1,0:T(8,128)(2,1)S(1)}, bf16[1,2,5,1,256,128]{5,4,3,2,1,0:T(8,128)(2,1)S(1)}) fusion(bf16[2,2,5,1,256,128]{5,4,3,2,1,0:T(8,128)(2,1)} %param.3), kind=kLoop, calls=%fused_computation.342 | loop fusion | bytes 2621440 | tf_op jit(solution)/shard_map/slice | solution.py:53
  11.7 0.1 convert_multiply_fusion
  11.8 0.3 fusion.2
  12.1 0.3 fusion.3
  12.4 0.6 add.598
  13.8 1.2 fusion.68
  15.0 0.4 fusion.66
  15.4 0.5 convolution_bitcast_fusion
  15.8 1.5 %convolution_bitcast_fusion.1 = f32[2560,128]{0,1:T(8,128)} fusion(bf16[2560,128]{1,0:T(8,128)(2,1)S(1)} %bitcast.111, s32[]{:T(128)} %bitcast, s32[128]{0:T(128)S(1)} %broadcast_multiply_fusion.3), kind=kOutput, calls=%fused_computation.1 | convolution fusion | flops 84197376 | bytes 1966596 | tf_op jit(solution)/shard_map/dot_general | solution.py:62
  17.5 0.1 copy.23
  17.6 0.6 convolution_bitcast_fusion.5
  18.3 0.3 convolution_bitcast_fusion.7
  18.6 0.1 reshape.486
  18.7 0.6 convolution_bitcast_fusion.4
  19.3 0.3 convolution_bitcast_fusion.6
  19.6 0.1 reshape.489
  19.8 1.5 %copy.24 = f32[2560,128]{1,0:T(8,128)} copy(f32[2560,128]{0,1:T(8,128)S(1)} %convolution_bitcast_fusion) | data formatting | bytes 2621440 | tf_op jit(solution)/shard_map/dot_general | solution.py:62
  21.2 1.5 %copy.22 = f32[2560,128]{1,0:T(8,128)} copy(f32[2560,128]{0,1:T(8,128)S(1)} %copy-done) | data formatting | bytes 2621440 | tf_op jit(solution)/shard_map/dot_general | solution.py:62
  22.7 1.7 %multiply_reduce_fusion = (f32[256,128]{1,0:T(8,128)S(1)}, f32[10,128]{1,0:T(8,128)S(1)}, f32[10,128]{1,0:T(8,128)S(1)}, f32[256,128]{1,0:T(8,128)S(1)}) fusion(f32[10,1,256,128]{3,2,0,1:T(8,128)S(1)} %bitcast.115, f32[10,128]{1,0:T(8,128)S(1)} %get-tuple-element.23, f32[256,128]{1,0:T(8,128)S(1)} %copy.23, f32[10,1,256,128]{3,2,0,1:T(8,128)} %bitcast.116, ...), kind=kLoop, calls=%fused_computation.2 | loop fusion | flops 2553344 | bytes 3035136 | tf_op jit(solution)/shard_map/reduce_sum | solution.py:70
  24.4 0.1 fusion.70
  24.6 13.2 %all-reduce = (f32[1,128]{1,0:T(1,128)S(1)}, f32[2304,2,1]{0,1,2:T(2,128)S(1)}, f32[2304,2,1]{0,1,2:T(2,128)S(1)}) all-reduce(f32[1,128]{1,0:T(1,128)S(1)} %add_bitcast_fusion, f32[2304,2,1]{0,1,2:T(2,128)S(1)} %reshape.486, f32[2304,2,1]{0,1,2:T(2,128)S(1)} %reshape.489), channel_id=1, replica_groups=mesh['groups'=2,'gx'=4,'gz'=2,'vert'=2] {'gz','vert'}, use_global_device_ids=true, to_apply=%region_2.0 | all-reduce | flops 9344 | bytes 74752 | tf_op jit(solution)/shard_map/psum | solution.py:82
  37.7 1.5 %copy.28 = f32[2304,2,1]{1,2,0:T(1,128)S(1)} copy(f32[2304,2,1]{0,1,2:T(2,128)S(1)} %get-tuple-element.9) | data formatting | bytes 36864 | tf_op jit(solution)/shard_map/psum | solution.py:82
  39.2 0.5 broadcast.1041
  39.8 10.4 %reduce.10 = f32[2304,2]{1,0:T(8,128)S(1)} reduce(f32[2304,1,2]{2,1,0:T(1,128)S(1)} %bitcast.117, f32[]{:T(128)} %broadcast.1041), dimensions={1}, to_apply=%bitcast.99.reduce_sub_computation | reduce | bytes 36868
  50.2 1.3 %reshape.496 = f32[4,1,1152]{2,1,0:T(1,128)} reshape(f32[2304,2]{1,0:T(8,128)S(1)} %reduce.10) | data formatting | bytes 36864
  51.5 4.9 %all-to-all-start = ((f32[4,1,1152]{2,1,0:T(1,128)}), f32[4,1,1152]{2,1,0:T(1,128)S(1)}, u32[]{:S(2)}, u32[]{:S(2)}) async-start(f32[4,1,1152]{2,1,0:T(1,128)} %reshape.496), calls=%async_computation | async-start | bytes 36864 | tf_op jit(solution)/shard_map/all_to_all | solution.py:88
  56.4 0.7 add.597
  57.1 0.5 broadcast_multiply_fusion.2
  57.6 1.4 %copy.33 = f32[2304,2,1]{1,2,0:T(1,128)S(1)} copy(f32[2304,2,1]{0,1,2:T(2,128)S(1)} %get-tuple-element.10) | data formatting | bytes 36864 | tf_op jit(solution)/shard_map/psum | solution.py:82
  59.1 10.4 %reduce.12 = f32[2304,2]{1,0:T(8,128)S(1)} reduce(f32[2304,1,2]{2,1,0:T(1,128)S(1)} %bitcast.118, f32[]{:T(128)} %broadcast.1041), dimensions={1}, to_apply=%bitcast.101.reduce_sub_computation | reduce | bytes 36868
  69.5 1.3 %reshape.498 = f32[4,1,1152]{2,1,0:T(1,128)} reshape(f32[2304,2]{1,0:T(8,128)S(1)} %reduce.12) | data formatting | bytes 36864
  70.8 5.1 %all-to-all-start.1 = ((f32[4,1,1152]{2,1,0:T(1,128)}), f32[4,1,1152]{2,1,0:T(1,128)S(1)}, u32[]{:S(2)}, u32[]{:S(2)}) async-start(f32[4,1,1152]{2,1,0:T(1,128)} %reshape.498), calls=%async_computation.1 | async-start | bytes 36864 | tf_op jit(solution)/shard_map/all_to_all | solution.py:88
  75.9 0.7 reduce.11
  76.6 1.8 %reshape.497 = f32[2304,1,2]{2,1,0:T(1,128)S(1)} reshape(f32[4,1152]{1,0:T(4,128)S(1)} %reduce.11) | data formatting | bytes 36864
  78.5 0.4 copy.35
  78.9 2.7 %all-to-all-done.1 = f32[4,1,1152]{2,1,0:T(1,128)S(1)} async-done(((f32[4,1,1152]{2,1,0:T(1,128)}), f32[4,1,1152]{2,1,0:T(1,128)S(1)}, u32[]{:S(2)}, u32[]{:S(2)}) %all-to-all-start.1) | async-done | bytes 18464 | tf_op jit(solution)/shard_map/all_to_all | solution.py:88
  81.5 0.7 reduce.13
  82.2 1.8 %reshape.499 = f32[2304,1,2]{2,1,0:T(1,128)S(1)} reshape(f32[4,1152]{1,0:T(4,128)S(1)} %reduce.13) | data formatting | bytes 36864
  84.1 0.4 copy.36
  84.5 0.3 fusion.64
  84.8 1.0 fusion.4
  85.8 1.3 %broadcast_multiply_fusion = f32[128,16]{0,1:T(8,128)} fusion(f32[128,16]{0,1:T(8,128)} %reduce-scatter.5.cloned.1.call-done), kind=kLoop, calls=%fused_computation.117 | loop fusion | flops 2048 | bytes 16384 | tf_op jit(solution)/shard_map/mul | solution.py:105
  87.1 29.7 %reduce-scatter.3.cloned.1.call-done = f32[16,128]{1,0:T(8,128)} async-done(((f32[256,128]{1,0:T(8,128)}), f32[16,128]{1,0:T(8,128)}) %reduce-scatter.3.cloned.1.call-update) | async-done | bytes 8208 | tf_op jit(solution)/shard_map/reduce_scatter | solution.py:93
  116.8 1.3 %broadcast_multiply_fusion.1 = f32[16,128]{1,0:T(8,128)} fusion(f32[16,128]{1,0:T(8,128)} %reduce-scatter.3.cloned.1.call-done), kind=kLoop, calls=%fused_computation.118 | loop fusion | flops 2048 | bytes 16384 | tf_op jit(solution)/shard_map/mul | solution.py:105
  (26 shorter events, 0.6 us)
Async XLA Ops:
  7.2 78.7 %reduce-scatter.5.cloned.1.call-start = ((), (), s32[]{:S(2)}) async-start(), calls=%async_computation.5 | async-start | bytes 73728 | tf_op jit(solution)/shard_map/reduce_scatter | solution.py:92
  15.8 1.8 %copy-start.2 = (f32[48,2560]{1,0:T(8,128)S(1)}, f32[48,2560]{1,0:T(8,128)}, u32[]{:S(2)}) copy-start(f32[48,2560]{1,0:T(8,128)} %fusion.68) | copy-start | bytes 1474564
  19.7 1.5 %copy-start = (f32[2560,128]{0,1:T(8,128)S(1)}, f32[2560,128]{0,1:T(8,128)}, u32[]{:S(2)}) copy-start(f32[2560,128]{0,1:T(8,128)} %convolution_bitcast_fusion.1) | copy-start | bytes 3932164
  21.2 1.5 %copy-start.1 = (f32[2560,128]{1,0:T(8,128)S(1)}, f32[2560,128]{1,0:T(8,128)}, u32[]{:S(2)}) copy-start(f32[2560,128]{1,0:T(8,128)} %copy.24) | copy-start | bytes 3932164
  51.5 19.3 %all-to-all-start = ((f32[4,1,1152]{2,1,0:T(1,128)}), f32[4,1,1152]{2,1,0:T(1,128)S(1)}, u32[]{:S(2)}, u32[]{:S(2)}) async-start(f32[4,1,1152]{2,1,0:T(1,128)} %reshape.496), calls=%async_computation | async-start | bytes 36864 | tf_op jit(solution)/shard_map/all_to_all | solution.py:88
  56.4 60.4 %reduce-scatter.3.cloned.1.call-start = ((), (), s32[]{:S(2)}) async-start(), calls=%async_computation.4 | async-start | bytes 139264 | tf_op jit(solution)/shard_map/reduce_scatter | solution.py:93
  70.8 10.7 %all-to-all-start.1 = ((f32[4,1,1152]{2,1,0:T(1,128)}), f32[4,1,1152]{2,1,0:T(1,128)S(1)}, u32[]{:S(2)}, u32[]{:S(2)}) async-start(f32[4,1,1152]{2,1,0:T(1,128)} %reshape.498), calls=%async_computation.1 | async-start | bytes 36864 | tf_op jit(solution)/shard_map/all_to_all | solution.py:88
Sparse Core Ops, SparseCore 0:
  13.2 32.7 reduce-scatter.4
  61.1 55.6 reduce-scatter.2
where the time goes:
time: 125 us
  waiting for transfers between devices  32.4 us (26%)
  other arithmetic  29.6 us (24%)
  local copies, waits for them, and re-layouts  16.8 us (13%)
  between operations  15.6 us (12%)
  blocking collectives  13.2 us (11%)
  starting transfers between devices  10 us (8%)
  matrix products  7.37 us (6%)
    reduce_scatter x1, waiting for transfers between devices, finish(): lax.psum_scatter(part_y, ('gx', 'gz', 'vert'), scatter_dimension=0, tiled...  29.7 us
    unnamed x2, other arithmetic  20.9 us
    psum x1, blocking collectives, finish(): summed, sum_x = lax.psum((partial_core, part_x), ('gz', 'vert'))  13.2 us
    all_to_all x2, starting transfers between devices, finish(): lax.all_to_all(summed, 'gx', split_axis=0, concat_axis=2, tiled=True)  9.97 us
    unnamed x11, local copies, waits for them, and re-layouts  6.86 us
    dot_general x2, local copies, waits for them, and re-layouts, batch_terms(): jnp.dot(rows_z, az_low, preferred_element_type=jnp.float32)  2.95 us
    psum x2, local copies, waits for them, and re-layouts, finish(): summed, sum_x = lax.psum((partial_core, part_x), ('gz', 'vert'))  2.89 us
    all_to_all x2, waiting for transfers between devices, finish(): lax.all_to_all(summed, 'gx', split_axis=0, concat_axis=2, tiled=True)  2.68 us
  transfers between devices with their start and end apart: 4, of which 2 were waited for; matrix products, arithmetic and copies ran while one was open for 38% of the time, Pallas kernels for 0%

commit v1 on v0

--- a/solution.py
+++ b/solution.py
@@ -1,8 +1,11 @@
+import functools
 import math
 
 import jax
 import jax.numpy as jnp
 from jax import lax
+from jax.experimental import pallas as pl
+from jax.experimental.pallas import tpu as pltpu
 from jax.sharding import PartitionSpec as P
 
 K = 128
@@ -28,7 +31,7 @@
     return unit_value(row_ids[:, None] * stride + col_ids[None, :], stream, salt)
 
 
-def shards(flow_field, test_streams, snapshot_ids):
+def shards_general(flow_field, test_streams, snapshot_ids):
     highest = lax.Precision.HIGHEST
     batches, local_snaps, variables, cells_x, cells_y, cells_z = flow_field.shape
     slabs_x = lax.axis_size("gx")
@@ -105,6 +108,369 @@
     return (totals[0] * scale_x, totals[1] * scale_y, totals[2] * scale_z, totals[3] * scale_core)
 
 
+MESH = pl.DeviceIdType.MESH
+PAD = 16
+
+
+def iota(shape, dim):
+    return lax.broadcasted_iota(jnp.int32, shape, dim)
+
+
+def unit_f32(index, stream, salt):
+    return unit_value(index, stream, salt).astype(jnp.float32)
+
+
+def dot_f32(left, right):
+    return jnp.dot(left, right, preferred_element_type=jnp.float32)
+
+
+def dot_split(left, right):
+    upper = left.astype(jnp.bfloat16)
+    lower = (left - upper.astype(jnp.float32)).astype(jnp.bfloat16)
+    return dot_f32(upper, right) + dot_f32(lower, right)
+
+
+def sketch_kernel(
+    sizes,
+    streams,
+    snaps,
+    flow_hbm,
+    sums,
+    flow,
+    y_send,
+    y_got,
+    y_out,
+    y_in,
+    z_send,
+    z_got,
+    z_out,
+    z_in,
+    c_send,
+    c_got,
+    c_out,
+    c_in,
+    load_sem,
+    pair_send,
+    pair_recv,
+    y_ssem,
+    y_rsem,
+    c_ssem,
+    c_rsem,
+    z_ssem,
+    z_rsem,
+):
+    slabs, zsplit, pairs, variables, cells_y, cells_z = sizes
+    chips = slabs * zsplit
+    rows_y = cells_y // (2 * chips)
+    rows_z = K // (2 * slabs)
+    rows_m = S // slabs
+    total_z = cells_z * zsplit
+    gx = lax.axis_index("gx")
+    gz = lax.axis_index("gz")
+    vert = lax.axis_index("vert")
+    other = 1 - vert
+    offsets = [(dx, dz) for dx in range(slabs) for dz in range(zsplit)]
+
+    def target(dx, dz):
+        return {"gx": lax.rem(gx + dx, slabs), "gz": lax.rem(gz + dz, zsplit)}
+
+    barrier = pltpu.get_barrier_semaphore()
+    pl.semaphore_signal(barrier, inc=1, device_id={"vert": other}, device_id_type=MESH)
+    for dx, dz in offsets[1:]:
+        pl.semaphore_signal(barrier, inc=1, device_id=target(dx, dz), device_id_type=MESH)
+    loads = [
+        pltpu.make_async_copy(
+            flow_hbm.at[pl.ds(p * variables, variables)],
+            flow.at[pl.ds(p * variables, variables)],
+            load_sem.at[p],
+        )
+        for p in range(pairs)
+    ]
+    for load in loads:
+        load.start()
+
+    fac = streams[0]
+    cor = streams[1]
+    total_q = pairs * variables
+    q_rows = -(-total_q // 8) * 8
+
+    def run_ids(q_index):
+        ids = jnp.full(q_index.shape, 0, jnp.int32)
+        for p in range(pairs):
+            ids = jnp.where(q_index // variables == p, snaps[p], ids)
+        return ids * variables + lax.rem(q_index, variables)
+
+    z_base = gz * cells_z
+    az_tab = unit_value(
+        (z_base + iota((cells_z, K), 0)) * K + iota((cells_z, K), 1), fac, 3
+    )
+    r_rows = run_ids(iota((q_rows, K), 0))
+    aq_tab = unit_f32(r_rows * K + iota((q_rows, K), 1), fac, 4)
+    phq_tab = [unit_f32(r_rows * E + e, cor, 8) for e in range(E)]
+    ax_row = unit_f32(gx * K + iota((8, K), 1), fac, 1)[0:1]
+    ay_tab = unit_f32(iota((cells_y, K), 0) * K + iota((cells_y, K), 1), fac, 2)
+
+    wide = jnp.zeros((cells_y, K), jnp.float32)
+    for p in range(pairs):
+        loads[p].wait()
+        for v in range(variables):
+            q = p * variables + v
+            wide = wide + dot_f32(flow[q], az_tab) * aq_tab[q : q + 1]
+    x_row = jnp.sum(wide * ay_tab, axis=0, keepdims=True)
+    wide = wide * ax_row
+    for c in range(chips):
+        for v in range(2):
+            at = (2 * c + v) * rows_y
+            y_send[v, c] = wide[at : at + rows_y]
+
+    pl.semaphore_wait(barrier, chips)
+
+    def pair_copy(src, dst, which):
+        return pltpu.make_async_remote_copy(
+            src_ref=src,
+            dst_ref=dst,
+            send_sem=pair_send.at[which],
+            recv_sem=pair_recv.at[which],
+            device_id={"vert": other},
+            device_id_type=MESH,
+        )
+
+    pair_y = pair_copy(y_send.at[other], y_got, 0)
+    pair_y.start()
+
+    ay_turned = unit_value(iota((K, cells_y), 1) * K + iota((K, cells_y), 0), fac, 2)
+    rows_c = slabs * PAD
+    m_row = iota((rows_c, cells_y), 0)
+    m_ids = (m_row // PAD) * rows_m + lax.rem(m_row, PAD)
+    phy_tab = unit_value(m_ids * cells_y + iota((rows_c, cells_y), 1), cor, 6)
+    turned = jnp.concatenate([ay_turned, phy_tab], axis=0)
+    aq_turned = unit_f32(run_ids(iota((K, K), 1)) * K + iota((K, K), 0), fac, 4)
+    ax_turned = unit_f32(gx * K + iota((K, K), 0), fac, 1)
+    weights = aq_turned * ax_turned
+    lane = iota((cells_z, K), 1)
+    phz_tab = unit_f32((lane // E) * total_z + z_base + iota((cells_z, K), 0), cor, 7)
+    phz_tab = jnp.where(lane < E * S, phz_tab, 0.0)
+    phz_e = [
+        jnp.where(lax.rem(lane, E) == e, phz_tab, 0.0).astype(jnp.bfloat16) for e in range(E)
+    ]
+
+    copies = []
+    deep = jnp.zeros((K, cells_z), jnp.float32)
+    halves = [jnp.zeros((rows_c, cells_z), jnp.float32) for e in range(E)]
+    for q in range(total_q):
+        both = dot_f32(turned, flow[q])
+        deep = deep + both[:K] * weights[:, q : q + 1]
+        for e in range(E):
+            halves[e] = halves[e] + both[K:] * phq_tab[e][q : q + 1]
+        if q == total_q // 2:
+            pair_y.wait_recv()
+            y_out[...] = y_send[vert] + y_got[...]
+            for i, (dx, dz) in enumerate(offsets[1:]):
+                dest = target(dx, dz)
+                copy = pltpu.make_async_remote_copy(
+                    src_ref=y_out.at[dest["gx"] * zsplit + dest["gz"]],
+                    dst_ref=y_in.at[i],
+                    send_sem=y_ssem.at[i],
+                    recv_sem=y_rsem.at[i],
+                    device_id=dest,
+                    device_id_type=MESH,
+                )
+                copy.start()
+                copies.append(copy)
+    y_copies = list(copies)
+
+    for g in range(slabs):
+        for v in range(2):
+            at = (2 * g + v) * rows_z
+            z_send[v, g] = deep[at : at + rows_z]
+    pair_z = pair_copy(z_send.at[other], z_got, 1)
+    pair_z.start()
+    core = dot_split(halves[0], phz_e[0])
+    for e in range(1, E):
+        core = core + dot_split(halves[e], phz_e[e])
+    core = jnp.where(lax.rem(iota((rows_c, K), 0), PAD) == rows_m, x_row, core)
+    c_send[...] = core.reshape(slabs, PAD, K)
+    pair_c = pair_copy(c_send, c_got, 2)
+    pair_c.start()
+
+    z_copies = []
+    pair_z.wait_recv()
+    z_out[...] = z_send[vert] + z_got[...]
+    for dx in range(1, slabs):
+        to = lax.rem(gx + dx, slabs)
+        copy = pltpu.make_async_remote_copy(
+            src_ref=z_out.at[to],
+            dst_ref=z_in.at[dx - 1],
+            send_sem=z_ssem.at[dx - 1],
+            recv_sem=z_rsem.at[dx - 1],
+            device_id={"gx": to},
+            device_id_type=MESH,
+        )
+        copy.start()
+        z_copies.append(copy)
+    c_copies = []
+    pair_c.wait_recv()
+    c_out[...] = c_send[...] + c_got[...]
+    for i, (dx, dz) in enumerate(offsets[1:]):
+        dest = target(dx, dz)
+        copy = pltpu.make_async_remote_copy(
+            src_ref=c_out.at[dest["gx"]],
+            dst_ref=c_in.at[i],
+            send_sem=c_ssem.at[i],
+            recv_sem=c_rsem.at[i],
+            device_id=dest,
+            device_id_type=MESH,
+        )
+        copy.start()
+        c_copies.append(copy)
+
+    total = y_out[gx * zsplit + gz]
+    for i, copy in enumerate(y_copies):
+        copy.wait_recv()
+        total = total + y_in[i]
+    sums[0:rows_y, :] = total
+    total = z_out[gx]
+    for i, copy in enumerate(z_copies):
+        copy.wait_recv()
+        total = total + z_in[i]
+    sums[rows_y : rows_y + rows_z, :] = total
+    for dx in range(slabs):
+        total = c_out[gx] if dx == 0 else None
+        for dz in range(zsplit):
+            i = dx * zsplit + dz - 1
+            if i < 0:
+                continue
+            c_copies[i].wait_recv()
+            total = c_in[i] if total is None else total + c_in[i]
+        at = rows_y + rows_z + dx * PAD
+        sums[at : at + PAD, :] = total
+    for copy in [pair_y, pair_z, pair_c] + y_copies + z_copies + c_copies:
+        copy.wait_send()
+
+
+def finish_kernel(sizes, scales, streams, sums, out_x, out_y, out_z, out_core):
+    slabs, zsplit, pairs, variables, cells_y, cells_z = sizes
+    rows_y = cells_y // (2 * slabs * zsplit)
+    rows_z = K // (2 * slabs)
+    rows_m = S // slabs
+    gx = lax.axis_index("gx")
+    scale_x, scale_y, scale_z, scale_core = scales
+    top = rows_y + rows_z
+    out_y[...] = sums[0:rows_y, :] * scale_y
+    part_z = sums[rows_y:top, :] * scale_z
+    filler = jnp.zeros((K - rows_z, cells_z), jnp.float32)
+    out_z[...] = jnp.concatenate([part_z, filler], axis=0).T[:, :rows_z]
+    out_x[...] = sums[top + rows_m : top + rows_m + 1, :] * scale_x
+    rows_c = slabs * PAD
+    slot = iota((rows_c, K), 0)
+    x_ids = lax.rem(gx - slot // PAD + slabs, slabs)
+    phx = unit_f32(iota((rows_c, K), 1) * slabs + x_ids, streams[1], 5)
+    right = jnp.concatenate(
+        [jnp.where(lax.rem(slot, PAD) == m, phx, 0.0).astype(jnp.bfloat16) for m in range(rows_m)],
+        axis=1,
+    )
+    left = (sums[top : top + rows_c, :] * scale_core).T
+    result = dot_split(left, right)
+    for m in range(rows_m):
+        out_core[m * E * S : (m + 1) * E * S, :] = result[: E * S, m * K : m * K + S]
+
+
+def shards_fused(sizes, flow_field, test_streams, snapshot_ids):
+    slabs, zsplit, pairs, variables, cells_y, cells_z = sizes
+    chips = slabs * zsplit
+    rows_y = cells_y // (2 * chips)
+    rows_z = K // (2 * slabs)
+    rows_m = S // slabs
+    rows_c = slabs * PAD
+    total_q = pairs * variables
+    rows = rows_y + rows_z + rows_c
+    f32 = jnp.float32
+    smem = pl.BlockSpec(memory_space=pltpu.SMEM)
+    vmem = pl.BlockSpec(memory_space=pltpu.VMEM)
+    dma = pltpu.SemaphoreType.DMA
+    sums = pl.pallas_call(
+        functools.partial(sketch_kernel, sizes),
+        name="sketch",
+        out_shape=jax.ShapeDtypeStruct((rows, K), f32),
+        in_specs=[smem, smem, pl.BlockSpec(memory_space=pl.ANY)],
+        out_specs=vmem,
+        scratch_shapes=[
+            pltpu.VMEM((total_q, cells_y, cells_z), jnp.bfloat16),
+            pltpu.VMEM((2, chips, rows_y, K), f32),
+            pltpu.VMEM((chips, rows_y, K), f32),
+            pltpu.VMEM((chips, rows_y, K), f32),
+            pltpu.VMEM((chips - 1, rows_y, K), f32),
+            pltpu.VMEM((2, slabs, rows_z, cells_z), f32),
+            pltpu.VMEM((slabs, rows_z, cells_z), f32),
+            pltpu.VMEM((slabs, rows_z, cells_z), f32),
+            pltpu.VMEM((slabs - 1, rows_z, cells_z), f32),
+            pltpu.VMEM((slabs, PAD, K), f32),
+            pltpu.VMEM((slabs, PAD, K), f32),
+            pltpu.VMEM((slabs, PAD, K), f32),
+            pltpu.VMEM((chips - 1, PAD, K), f32),
+            dma((pairs,)),
+            dma((3,)),
+            dma((3,)),
+            dma((chips - 1,)),
+            dma((chips - 1,)),
+            dma((chips - 1,)),
+            dma((chips - 1,)),
+            dma((slabs - 1,)),
+            dma((slabs - 1,)),
+        ],
+        compiler_params=pltpu.CompilerParams(
+            collective_id=0, has_side_effects=True, vmem_limit_bytes=24 * 2**20
+        ),
+    )(
+        test_streams,
+        snapshot_ids.reshape(pairs),
+        flow_field.reshape(total_q, cells_y, cells_z),
+    )
+    total_x = slabs
+    total_z = cells_z * zsplit
+    all_q = 2 * total_q
+    scales = (
+        3.0**1.5 / math.sqrt(cells_y * total_z * all_q),
+        3.0**1.5 / math.sqrt(total_x * total_z * all_q),
+        3.0**1.5 / math.sqrt(total_x * cells_y * all_q),
+        9.0 / math.sqrt(total_x * cells_y * total_z * all_q),
+    )
+    out_x, out_y, out_z, out_core = pl.pallas_call(
+        functools.partial(finish_kernel, sizes, scales),
+        name="finish",
+        out_shape=[
+            jax.ShapeDtypeStruct((1, K), f32),
+            jax.ShapeDtypeStruct((rows_y, K), f32),
+            jax.ShapeDtypeStruct((cells_z, rows_z), f32),
+            jax.ShapeDtypeStruct((rows_m * S * E, S), f32),
+        ],
+        in_specs=[smem, vmem],
+        out_specs=[vmem, vmem, vmem, vmem],
+        compiler_params=pltpu.CompilerParams(vmem_limit_bytes=24 * 2**20),
+    )(test_streams, sums)
+    return (out_x, out_y, out_z, out_core.reshape(rows_m * S, E, S))
+
+
+def shards(flow_field, test_streams, snapshot_ids):
+    batches, local_snaps, variables, cells_x, cells_y, cells_z = flow_field.shape
+    slabs = lax.axis_size("gx")
+    zsplit = lax.axis_size("gz")
+    fits = (
+        lax.axis_size("vert") == 2
+        and cells_x == 1
+        and cells_z == K
+        and cells_y % (16 * slabs * zsplit) == 0
+        and K % (16 * slabs) == 0
+        and S % slabs == 0
+        and S // slabs < PAD
+        and batches * local_snaps * variables <= K
+    )
+    if not fits:
+        return shards_general(flow_field, test_streams, snapshot_ids)
+    sizes = (slabs, zsplit, batches * local_snaps, variables, cells_y, cells_z)
+    return shards_fused(sizes, flow_field, test_streams, snapshot_ids)
+
+
 def solution(mesh):
     in_specs = (P("groups", "vert", None, "gx", None, "gz"), P("groups"), P("groups", "vert"))
     out_specs = (

time: 125 us -> 19.9 us (0.16)
  waiting for transfers between devices: 32.4 us -> 0 us
  other arithmetic: 29.6 us -> 0 us
  between operations: 15.6 us -> 0.64 us
  Pallas kernels: 0 us -> 14.8 us
  blocking collectives: 13.2 us -> 0 us
  local copies, waits for them, and re-layouts: 16.8 us -> 4.31 us
  starting transfers between devices: 10 us -> 0 us
  matrix products: 7.37 us -> 0 us
    reduce_scatter x2 -> x0, waiting for transfers between devices: 29.7 us -> none  [the longest x1 29.7 us: finish(): lax.psum_scatter(part_y, ('gx', 'gz', 'vert'), scatter_dimension=0, tiled...]
    unnamed x2 -> x0, other arithmetic: 20.9 us -> none
    pallas_call x0 -> x2, Pallas kernels: none -> 14.8 us  [the longest x1 13.3 us: shards_fused(): pl.pallas_call(functools.partial(sketch_kernel, sizes), name='sketch', ou...]
    psum x1 -> x0, blocking collectives: 13.2 us -> none  [finish(): summed, sum_x = lax.psum((partial_core, part_x), ('gz', 'vert'))]
    all_to_all x2 -> x0, starting transfers between devices: 9.97 us -> none  [finish(): lax.all_to_all(summed, 'gx', split_axis=0, concat_axis=2, tiled=True)]
    dot_general x12 -> x0, matrix products: 7.37 us -> none  [the longest x2 2 us: batch_terms(): jnp.dot(rows_z, az_low, preferred_element_type=jnp.float32)]
    mul x11 -> x0, other arithmetic: 4.11 us -> none  [the longest x1 1.3 us: shards(): totals[2] * scale_z]
    unnamed x11 -> x6, local copies, waits for them, and re-layouts: 6.86 us -> 3.55 us
  transfers between devices with their start and end apart: 4 -> 0, of which waited for: 2 -> 0; matrix products, arithmetic and copies ran while one was open for 38% -> 0% of each run, Pallas kernels for 0% -> 0%
where the time goes in v1:
time: 19.9 us; the launch traced here: 19.7 us
  Pallas kernels  14.8 us (74%)
  local copies, waits for them, and re-layouts  4.31 us (22%)
  between operations  0.64 us (3%)
    pallas_call x1, Pallas kernels, shards_fused(): pl.pallas_call(functools.partial(sketch_kernel, sizes), name='sketch', ou...  13.3 us
    unnamed x6, local copies, waits for them, and re-layouts  3.55 us
    pallas_call x1, Pallas kernels, shards_fused(): pl.pallas_call(functools.partial(finish_kernel, sizes, scales), name='fin...  1.46 us
    reshape x1, local copies, waits for them, and re-layouts, shards_fused(): snapshot_ids.reshape(pairs)  0.76 us

profile of v1, /device:TPU:0, one launch (start us, length us, event | category | flops | bytes accessed | tf_op | source)
XLA Modules:
  0.0 19.7 jit_solution(840384037438390752)
XLA Ops:
  0.6 0.8 %reshape.17.snaps = s32[4]{0:T(128)S(1)} reshape(s32[2,2]{1,0:T(2,128)} %param.5) | data formatting | bytes 32 | tf_op jit(solution)/shard_map/reshape | solution.py:426
  1.4 0.0 copy-start
  1.4 1.3 %copy-done = bf16[2,2,5,1,256,128]{5,4,3,2,1,0:T(8,128)(2,1)S(1)} copy-done((bf16[2,2,5,1,256,128]{5,4,3,2,1,0:T(8,128)(2,1)S(1)}, bf16[2,2,5,1,256,128]{5,4,3,2,1,0:T(8,128)(2,1)}, u32[]{:S(2)}) %copy-start) | copy-done | bytes 1310744
  2.7 0.0 copy-start.1
  2.7 0.7 %copy-done.1 = s32[2]{0:T(128)S(1)} copy-done((s32[2]{0:T(128)S(1)}, s32[2]{0:T(128)}, u32[]{:S(2)}) %copy-start.1) | copy-done | bytes 32
  3.4 13.3 %sketch.1.sums = f32[96,128]{1,0:T(8,128)S(1)} custom-call(s32[2]{0:T(128)S(1)} %copy-done.1, s32[4]{0:T(128)S(1)} %reshape.17.snaps, bf16[20,256,128]{2,1,0:T(8,128)(2,1)S(1)} %bitcast.2), custom_call_target="tpu_custom_call" | custom-call | tf_op jit(solution)/shard_map/sketch/pallas_call | solution.py:391
  16.7 1.5 %finish.1 = (f32[1,128]{1,0:T(1,128)}, f32[16,128]{1,0:T(8,128)}, f32[128,16]{1,0:T(8,128)S(1)}, f32[1152,48]{1,0:T(8,128)S(1)}) custom-call(s32[2]{0:T(128)S(1)} %copy-done.1, f32[96,128]{1,0:T(8,128)S(1)} %sketch.1.sums), custom_call_target="tpu_custom_call" | custom-call | tf_op jit(solution)/shard_map/finish/pallas_call | solution.py:438
  18.2 0.7 %copy.7 = f32[128,16]{0,1:T(8,128)} copy(f32[128,16]{1,0:T(8,128)S(1)} %get-tuple-element.14) | data formatting | bytes 16384
  18.8 0.9 %copy.8 = f32[576,2,48]{0,2,1:T(8,128)} copy(f32[576,2,48]{2,1,0:T(2,128)S(1)} %bitcast.3) | data formatting | bytes 442368
Async XLA Ops:
  1.4 1.3 %copy-start = (bf16[2,2,5,1,256,128]{5,4,3,2,1,0:T(8,128)(2,1)S(1)}, bf16[2,2,5,1,256,128]{5,4,3,2,1,0:T(8,128)(2,1)}, u32[]{:S(2)}) copy-start(bf16[2,2,5,1,256,128]{5,4,3,2,1,0:T(8,128)(2,1)} %param.3) | copy-start | bytes 3932164
  2.7 0.7 %copy-start.1 = (s32[2]{0:T(128)S(1)}, s32[2]{0:T(128)}, u32[]{:S(2)}) copy-start(s32[2]{0:T(128)} %streams.3) | copy-start | bytes 28
